TPU v7x, 32 devices: a whole 2x2x4 slice. The times are simulated.
32 devices in a mesh: tm: 8 (over z, x), feat: 2 (over core), rep: 2 (over y).
Axes of the slice: x: 2, y: 2, z: 4, core: 2. Of those that a mesh axis runs over, the one named last changes fastest.
Arguments:
- frames: bfloat16 [2, 2048, 16384], P('rep', 'tm', 'feat'), may hold values from -50 to 50, as said below
- panel_low: bfloat16 [16384, 512], P('feat', 'tm'), may hold values from -0.046875 to 0.046875
- panel_high: bfloat16 [16384, 512], P('feat', 'tm'), may hold values from -0.046875 to 0.046875
- lags: int32 [2], P('rep'), may hold values from 1 to 64, as said below
- seg_lengths: int32 [2, 64], P('rep'), may hold values from 1 to 256, 2048 in all within a row
- ridge: float32 [32], replicated, may hold values from 0.01 to 10
Outputs:
- covariances: float32 [3, 1024, 1024], P(None, ('tm', 'feat', 'rep'))
- scores: float32 [1024, 32], P(('tm', 'feat', 'rep'))
Inputs may be any that keep to these rules, and one draw needn't show every extreme that they name: The frames of each run follow one trajectory in time. `lags`: one run has the lag 64. `seg_lengths`: each row sums to 2048.
All inputs are finite; a program needn't handle non-finite values.
Results may differ from a plain program's by a relative error of at most 0.003.
Values may be sent and summed in bfloat16 or wider, within the bound.
A program may use at most 64 MiB of HBM per device.

v0:
```python
import jax
import jax.numpy as jnp
from jax import lax
from jax.sharding import PartitionSpec as P


def passed_along(shard, axis, by):
    length = lax.axis_size(axis)
    pairs = [(i, i + by) for i in range(length) if 0 <= i + by < length]
    return lax.ppermute(shard, axis, pairs)


def local(frames, panel_low, panel_high, lags, seg_lengths, ridge):
    local_frames = frames[0]
    t_local = local_frames.shape[0]
    lag_most = t_local // 4
    n_time = lax.axis_size("tm")
    n_feature = lax.axis_size("feat")
    n_replica = lax.axis_size("rep")
    panel_cols = panel_low.shape[1] * n_time
    basis_width = 2 * panel_cols
    per_device = basis_width // (n_time * n_feature * n_replica)
    time_index = lax.axis_index("tm")
    feature_index = lax.axis_index("feat")
    replica_index = lax.axis_index("rep")
    stacked = jnp.stack([panel_low, panel_high], axis=0)
    partial_sum = jnp.einsum(
        "tf,pfk->tpk",
        local_frames,
        lax.all_gather(stacked, "tm", axis=2, tiled=True),
        preferred_element_type=jnp.float32,
    )
    partial_sum = partial_sum.reshape(local_frames.shape[0], basis_width)
    partial_rounded = partial_sum.astype(jnp.bfloat16)
    summed = lax.psum(partial_rounded, "feat").astype(jnp.float32).astype(jnp.bfloat16)
    next_basis = passed_along(summed[:lag_most], "tm", -1)
    extended = jnp.concatenate([summed, next_basis], axis=0)
    lag_now = lags[0]
    lagged = lax.dynamic_slice_in_dim(extended, lag_now, t_local, 0)
    frame_total = t_local * n_time
    positions = time_index * t_local + jnp.arange(t_local, dtype=jnp.int32)
    seg_ends = jnp.cumsum(seg_lengths[0])
    end_of = jnp.min(
        jnp.where(seg_ends[None, :] > positions[:, None], seg_ends[None, :], frame_total), axis=1
    )
    keep_mask = (positions + lag_now < end_of).astype(jnp.bfloat16)[:, None]
    masked = summed * keep_mask
    lag_masked = lagged * keep_mask

    def own_group(values):
        shaped = values.reshape(t_local, n_time, n_feature, n_replica * per_device)
        return lax.dynamic_index_in_dim(shaped, feature_index, 2, keepdims=False).reshape(
            t_local, -1
        )

    group_masked = own_group(masked)
    group_lagged = own_group(lag_masked)
    term_inst = jnp.einsum("ti,tj->ij", group_masked, summed, preferred_element_type=jnp.float32)
    term_cross = jnp.einsum("ti,tj->ij", group_masked, lagged, preferred_element_type=jnp.float32)
    term_lagged = jnp.einsum("ti,tj->ij", group_lagged, lagged, preferred_element_type=jnp.float32)
    row_block = lax.psum_scatter(
        jnp.stack([term_inst, term_cross, term_lagged], axis=1),
        ("tm", "rep"),
        scatter_dimension=0,
        tiled=True,
    )
    inverse_count = 1.0 / (frame_total * n_replica)
    cov_rows = jnp.transpose(row_block, (1, 0, 2)) * inverse_count
    device_linear = (time_index * n_feature + feature_index) * n_replica + replica_index
    own_index = device_linear * per_device + jnp.arange(per_device, dtype=jnp.int32)
    selector = (jnp.arange(basis_width, dtype=jnp.int32)[None, :] == own_index[:, None]).astype(
        jnp.float32
    )
    diag_inst = jnp.sum(cov_rows[0] * selector, axis=1)
    local_var = jnp.sum(jnp.square(lag_masked.astype(jnp.float32)), axis=0)
    diag_lagged = lax.psum(local_var, ("tm", "rep")) * inverse_count
    inverse_lagged = 1.0 / (diag_lagged[:, None] + ridge[None, :])
    weighted = jnp.dot(
        jnp.square(cov_rows[1]),
        inverse_lagged,
        precision=lax.Precision.HIGHEST,
        preferred_element_type=jnp.float32,
    )
    scores = weighted / (diag_inst[:, None] + ridge[None, :])
    return (cov_rows, scores)


def solution(mesh):
    in_specs = (
        P("rep", "tm", "feat"),
        P("feat", "tm"),
        P("feat", "tm"),
        P("rep"),
        P("rep", None),
        P(),
    )
    out_specs = (P(None, ("tm", "feat", "rep"), None), P(("tm", "feat", "rep"), None))
    return jax.shard_map(local, mesh=mesh, in_specs=in_specs, out_specs=out_specs, check_vma=False)
```

profile of v0, /device:TPU:0, one launch (start us, length us, event | category | flops | bytes accessed | tf_op | source)
XLA Modules:
  0.0 433.6 jit_solution(18083150070705412241)
XLA Ops:
  7.2 0.0 all-gather.2.cloned.1.call-start
  7.2 3.1 pad_maximum_fusion.1
  10.3 0.0 all-gather.2.cloned.1.call-update
  10.3 0.0 copy-start.2
  10.3 0.0 all-reduce.2.cloned.1.call-start
  10.4 230.4 %all-gather.2.cloned.1.call-done = bf16[2,8192,512]{1,2,0:T(8,128)(2,1)} async-done(((bf16[2,8192,64]{1,2,0:T(8,128)(2,1)}), bf16[2,8192,512]{1,2,0:T(8,128)(2,1)}) %all-gather.2.cloned.1.call-update) | async-done | bytes 16777232 | tf_op jit(solution)/shard_map/all_gather | solution.py:30
  240.8 12.3 %fusion.2 = bf16[2,512,256]{2,1,0:T(8,128)(2,1)} fusion(bf16[2,8192,512]{1,2,0:T(8,128)(2,1)} %all-gather.2.cloned.1.call-done, bf16[1,256,8192]{2,1,0:T(8,128)(2,1)} %param.6), kind=kOutput, calls=%fused_computation.7 | convolution fusion | flops 4295229440 | bytes 21495808 | tf_op jit(solution)/shard_map/tf,pfk->tpk/dot_general | solution.py:27
  253.0 0.0 all-reduce.2.cloned.1.call-update
  253.1 0.0 reduce-scatter.2.cloned.1.call-start
  253.8 0.0 copy-done.2
  253.8 0.1 copy.10
  253.9 0.1 reduce-window.8
  254.0 0.1 reduce
  254.1 0.1 select_reduce_fusion
  254.2 15.9 %all-reduce.2.cloned.1.call-done = bf16[256,1024]{0,1:T(8,128)(2,1)} async-done(((bf16[256,1024]{0,1:T(8,128)(2,1)}), bf16[256,1024]{0,1:T(8,128)(2,1)}) %all-reduce.2.cloned.1.call-update) | async-done | bytes 524304 | tf_op jit(solution)/shard_map/psum | solution.py:35
  270.1 1.0 slice.12
  271.2 1.3 collective-permute-start
  272.5 1.1 broadcast_multiply_fusion.1
  273.6 1.5 convolution_bitcast_fusion.2
  275.1 6.5 %collective-permute-done = bf16[64,1024]{0,1:T(8,128)(2,1)S(1)} collective-permute-done((bf16[64,1024]{0,1:T(8,128)(2,1)S(1)}, bf16[64,1024]{0,1:T(8,128)(2,1)S(1)}, u32[]{:S(2)}, u32[]{:S(2)}) %collective-permute-start) | collective-permute-done | bytes 131104 | tf_op jit(solution)/shard_map/ppermute | solution.py:10
  281.6 0.0 copy-done
  281.6 0.7 multiply_reduce_fusion
  282.3 0.5 convolution_bitcast_fusion.1
  282.8 0.5 convolution_bitcast_fusion
  283.3 3.2 pad_maximum_fusion
  286.5 0.0 reduce-scatter.2.cloned.1.call-update
  286.6 41.0 %psum.15 = f32[1024]{0:T(1024)S(1)} all-reduce(f32[1024]{0:T(1024)S(1)} %get-tuple-element.2), channel_id=1, replica_groups=mesh['tm'=8,'feat'=2,'rep'=2] {'tm','rep'}, use_global_device_ids=true, to_apply=%region_5.6 | all-reduce | flops 1024 | bytes 8192 | tf_op jit(solution)/shard_map/psum | solution.py:76
  327.6 97.1 %reduce-scatter.2.cloned.1.call-done = f32[32,3,1024]{2,0,1:T(8,128)} async-done(((f32[512,3,1024]{2,0,1:T(8,128)}), f32[32,3,1024]{2,0,1:T(8,128)}) %reduce-scatter.2.cloned.1.call-update) | async-done | bytes 393232 | tf_op jit(solution)/shard_map/reduce_scatter | solution.py:61
  424.7 1.0 multiply_bitcast_fusion
  425.7 0.0 copy-start.1
  425.7 0.2 fusion.10
  425.9 1.1 convolution_divide_fusion
  (10 shorter events, 0.1 us)
Async XLA Ops:
  7.2 233.6 %all-gather.2.cloned.1.call-start = ((), (), s32[]{:S(2)}) async-start(), calls=%async_computation.1 | async-start | bytes 18874368 | tf_op jit(solution)/shard_map/all_gather | solution.py:30
  10.3 243.5 %copy-start.2 = (s32[1,64]{1,0:T(1,128)S(1)}, s32[1,64]{1,0:T(1,128)}, u32[]{:S(2)}) copy-start(s32[1,64]{1,0:T(1,128)} %param.10) | copy-start | bytes 772
  10.3 259.8 %all-reduce.2.cloned.1.call-start = ((), (), s32[]{:S(2)}) async-start(), calls=%async_computation.2 | async-start | bytes 1048576 | tf_op jit(solution)/shard_map/psum | solution.py:35
  253.1 171.6 %reduce-scatter.2.cloned.1.call-start = ((), (), s32[]{:S(2)}) async-start(), calls=%async_computation.3 | async-start | bytes 6684672 | tf_op jit(solution)/shard_map/reduce_scatter | solution.py:61
  270.1 11.4 %copy-start = (bf16[256,1024]{0,1:T(8,128)(2,1)S(1)}, bf16[256,1024]{0,1:T(8,128)(2,1)}, u32[]{:S(2)}) copy-start(bf16[256,1024]{0,1:T(8,128)(2,1)} %all-reduce.2.cloned.1.call-done) | copy-start | bytes 1572868
  271.2 10.4 %collective-permute-start = (bf16[64,1024]{0,1:T(8,128)(2,1)S(1)}, bf16[64,1024]{0,1:T(8,128)(2,1)S(1)}, u32[]{:S(2)}, u32[]{:S(2)}) collective-permute-start(bf16[64,1024]{0,1:T(8,128)(2,1)S(1)} %slice.12), channel_id=1, source_target_pairs={{4,0},{8,4},{12,8},{16,12},{20,16},{24,20},{28,24},{5,1},{9,5},{13... | collective-permute-start | bytes 393224 | tf_op jit(solution)/shard_map/ppermute | solution.py:10
  286.5 139.4 %copy-start.3 = (f32[32]{0:T(128)S(1)}, f32[32]{0:T(128)}, u32[]{:S(2)}) copy-start(f32[32]{0:T(128)} %param.11) | copy-start | bytes 388
  425.7 1.3 copy-start.1
Sparse Core Ops, SparseCore 0:
  10.4 230.2 all-gather.1
  253.2 16.8 all-reduce.1
  286.7 137.9 reduce-scatter.1
where the time goes:
time: 434 us
  waiting for transfers between devices  350 us (81%)
  blocking collectives  41 us (9%)
  matrix products  15.8 us (4%)
  between operations  14.5 us (3%)
  other arithmetic  9.67 us (2%)
    all_gather x1, waiting for transfers between devices, local(): lax.all_gather(stacked, 'tm', axis=2, tiled=True)  230 us
    reduce_scatter x1, waiting for transfers between devices, local(): lax.psum_scatter(jnp.stack([term_inst, term_cross, term_lagged], axis=1),...  97.1 us
    psum x1, blocking collectives, local(): diag_lagged = lax.psum(local_var, ('tm', 'rep')) * inverse_count  41 us
    psum x1, waiting for transfers between devices, local(): lax.psum(partial_rounded, 'feat').astype(jnp.float32).astype(jnp.bfloat16)  15.9 us
    dot_general x1, matrix products, local(): jnp.einsum('tf,pfk->tpk', local_frames, lax.all_gather(stacked, 'tm', axi...  12.3 us
  transfers between devices with their start and end apart: 4, of which 4 were waited for; matrix products, arithmetic and copies ran while one was open for 1% of the time, Pallas kernels for 0%

commit v1 on v0

--- a/solution.py
+++ b/solution.py
@@ -1,7 +1,13 @@
+import functools
 import jax
 import jax.numpy as jnp
 from jax import lax
+from jax.experimental import pallas as pl
+from jax.experimental.pallas import tpu as pltpu
 from jax.sharding import PartitionSpec as P
+
+MESH = pl.DeviceIdType.MESH
+TILE = 1024
 
 
 def passed_along(shard, axis, by):
@@ -10,7 +16,7 @@
     return lax.ppermute(shard, axis, pairs)
 
 
-def local(frames, panel_low, panel_high, lags, seg_lengths, ridge):
+def local_general(frames, panel_low, panel_high, lags, seg_lengths, ridge):
     local_frames = frames[0]
     t_local = local_frames.shape[0]
     lag_most = t_local // 4
@@ -66,14 +72,21 @@
     )
     inverse_count = 1.0 / (frame_total * n_replica)
     cov_rows = jnp.transpose(row_block, (1, 0, 2)) * inverse_count
-    device_linear = (time_index * n_feature + feature_index) * n_replica + replica_index
+    local_var = jnp.sum(jnp.square(lag_masked.astype(jnp.float32)), axis=0)
+    diag_lagged = lax.psum(local_var, ("tm", "rep")) * inverse_count
+    return finish(cov_rows, diag_lagged, ridge)
+
+
+def finish(cov_rows, diag_lagged, ridge):
+    per_device, basis_width = cov_rows.shape[1:]
+    device_linear = (
+        lax.axis_index("tm") * lax.axis_size("feat") + lax.axis_index("feat")
+    ) * lax.axis_size("rep") + lax.axis_index("rep")
     own_index = device_linear * per_device + jnp.arange(per_device, dtype=jnp.int32)
     selector = (jnp.arange(basis_width, dtype=jnp.int32)[None, :] == own_index[:, None]).astype(
         jnp.float32
     )
     diag_inst = jnp.sum(cov_rows[0] * selector, axis=1)
-    local_var = jnp.sum(jnp.square(lag_masked.astype(jnp.float32)), axis=0)
-    diag_lagged = lax.psum(local_var, ("tm", "rep")) * inverse_count
     inverse_lagged = 1.0 / (diag_lagged[:, None] + ridge[None, :])
     weighted = jnp.dot(
         jnp.square(cov_rows[1]),
@@ -83,6 +96,347 @@
     )
     scores = weighted / (diag_inst[:, None] + ridge[None, :])
     return (cov_rows, scores)
+
+
+def line_gather(n_z, z, chunks, slot, send_up, send_down, begin, ready, after_first, sems):
+    up_sem, down_sem, recv_sem = sems
+
+    def copy(place, k, sem, target):
+        return pltpu.make_async_remote_copy(
+            src_ref=slot(place, k), dst_ref=slot(place, k), send_sem=sem.at[place, k],
+            recv_sem=recv_sem.at[place, k], device_id=target, device_id_type=MESH)
+
+    for k in chunks:
+        begin(k)
+
+        @pl.when(z + 1 < n_z)
+        def _():
+            copy(z, k, up_sem, send_up).start()
+
+        @pl.when(z > 0)
+        def _():
+            copy(z, k, down_sem, send_down).start()
+
+        ready(z, k)
+    for step in range(1, n_z):
+        for k in chunks:
+            @pl.when(z - step >= 0)
+            def _():
+                place = z - step
+                copy(place, k, up_sem, send_up).wait_recv()
+
+                @pl.when(z + 1 < n_z)
+                def _():
+                    copy(place, k, up_sem, send_up).start()
+
+                ready(place, k)
+
+            @pl.when(z + step < n_z)
+            def _():
+                place = z + step
+                copy(place, k, down_sem, send_down).wait_recv()
+
+                @pl.when(z > 0)
+                def _():
+                    copy(place, k, down_sem, send_down).start()
+
+                ready(place, k)
+
+        if step == 1:
+            after_first()
+
+    def finish_sends():
+        for place in range(n_z):
+            for k in chunks:
+                @pl.when(jnp.logical_and(z + 1 < n_z, place <= z))
+                def _():
+                    copy(place, k, up_sem, send_up).wait_send()
+
+                @pl.when(jnp.logical_and(z > 0, place >= z))
+                def _():
+                    copy(place, k, down_sem, send_down).wait_send()
+
+    return finish_sends
+
+
+def kernel(n_time, frames_ref, low_ref, high_ref, out_ref, all_frames, all_panels, total, part, other,
+           y_out, y_in, local_sem, f_send, f_recv, p_up, p_down, p_recv, px_send, px_recv,
+           pz_send, pz_recv, c_send, c_recv, y_send, y_recv,
+           b_up, b_down, b_recv, bx_send, bx_recv, bc_send, bc_recv):
+    n_z = n_time // 2
+    tm, core, run = lax.axis_index("tm"), lax.axis_index("feat"), lax.axis_index("rep")
+    z, x = tm // 2, tm % 2
+    pair = z + 1 - 2 * (z % 2)
+    to_up = (jnp.minimum(tm + 2, n_time - 2 + x), core, run)
+    to_down = (jnp.maximum(tm - 2, x), core, run)
+    to_pair = (pair * 2 + x, core, run)
+    to_x = (z * 2 + (1 - x), core, run)
+    to_y = (tm, core, 1 - run)
+    to_core = (tm, 1 - core, run)
+    features = all_frames.shape[2]
+    cut = features // 2
+    chunks = range(4)
+    by_pair = (2, 3)
+
+    own_lanes = pl.ds(pl.multiple_of(run * features, features), features)
+    their_lanes = pl.ds(pl.multiple_of((1 - run) * features, features), features)
+    own_low = pltpu.make_async_copy(low_ref.at[:, own_lanes], all_panels.at[0, tm], local_sem.at[0])
+    own_high = pltpu.make_async_copy(high_ref.at[:, own_lanes], all_panels.at[1, tm], local_sem.at[1])
+    own_frames = pltpu.make_async_copy(
+        frames_ref.at[:, own_lanes], all_frames.at[run], local_sem.at[2])
+    own_low.start()
+    own_high.start()
+    own_frames.start()
+
+    barrier = pltpu.get_barrier_semaphore()
+
+    @pl.when(z + 1 < n_z)
+    def _():
+        pl.semaphore_signal(barrier, inc=1, device_id=to_up, device_id_type=MESH)
+
+    @pl.when(z > 0)
+    def _():
+        pl.semaphore_signal(barrier, inc=1, device_id=to_down, device_id_type=MESH)
+
+    for target in (to_x, to_y, to_core):
+        pl.semaphore_signal(barrier, inc=1, device_id=target, device_id_type=MESH)
+
+    @pl.when(jnp.logical_or(z == 0, z == n_z - 1))
+    def _():
+        pl.semaphore_wait(barrier, 4)
+
+    @pl.when(jnp.logical_and(z > 0, z < n_z - 1))
+    def _():
+        pl.semaphore_wait(barrier, 5)
+
+    def frame_copy(slot_run):
+        return pltpu.make_async_remote_copy(
+            src_ref=frames_ref.at[:, their_lanes], dst_ref=all_frames.at[slot_run],
+            send_sem=f_send.at[0], recv_sem=f_recv.at[0], device_id=to_y, device_id_type=MESH)
+
+    def panel_ref(place, side, k):
+        return all_panels.at[k // 2, place * 2 + side, :, pl.ds((k % 2) * cut, cut)]
+
+    def panel_slot(place, k):
+        return panel_ref(place, x, k)
+
+    def panel_x(place, side, k):
+        ref = panel_ref(place, side, k)
+        return pltpu.make_async_remote_copy(
+            src_ref=ref, dst_ref=ref, send_sem=px_send.at[place, k],
+            recv_sem=px_recv.at[place, k], device_id=to_x, device_id_type=MESH)
+
+    def panel_pair(place, k):
+        ref = panel_ref(place, 1 - x, k)
+        return pltpu.make_async_remote_copy(
+            src_ref=ref, dst_ref=ref, send_sem=pz_send.at[k], recv_sem=pz_recv.at[k],
+            device_id=to_pair, device_id_type=MESH)
+
+    def unless_by_pair(place, k, act):
+        if k in by_pair:
+            pl.when(place != pair)(act)
+        else:
+            act()
+
+    def panel_begin(k):
+        if k == 0:
+            own_low.wait()
+        if k == 2:
+            own_high.wait()
+
+    def panel_ready(place, k):
+        unless_by_pair(place, k, lambda: panel_x(place, x, k).start())
+
+    def pass_to_pair():
+        for k in by_pair:
+            panel_x(z, 1 - x, k).wait_recv()
+            panel_pair(z, k).start()
+
+    frame_copy(run).start()
+    panel_sends = line_gather(
+        n_z, z, chunks, panel_slot, to_up, to_down, panel_begin, panel_ready, pass_to_pair,
+        (p_up, p_down, p_recv))
+    own_frames.wait()
+    frame_copy(1 - run).wait_recv()
+    far = z // 2
+    rows, columns = total.shape
+    block = all_panels.shape[2] * 2
+    for turn, place in enumerate((z, pair, 2 - far, 3 - 3 * far)):
+        for k in chunks:
+            if turn == 0 and k in by_pair:
+                continue
+            if turn == 1 and k in by_pair:
+                panel_pair(place, k).wait_recv()
+            else:
+                panel_x(place, 1 - x, k).wait_recv()
+
+        def term(i, so_far):
+            at = pl.ds(pl.multiple_of(i * TILE, TILE), TILE)
+            left = all_frames[:, :, at].reshape(rows, TILE)
+            right = all_panels[:, pl.ds(place * 2, 2), :, at].reshape(2 * block, TILE)
+            return so_far + lax.dot_general(
+                left, right, (((1,), (1,)), ((), ())), preferred_element_type=jnp.float32)
+
+        result = lax.fori_loop(
+            0, features // TILE, term, jnp.zeros((rows, 2 * block), jnp.float32))
+        for panel in range(2):
+            at = pl.ds(pl.multiple_of(panel * (columns // 2) + place * block, block), block)
+            total[:, at] = result[:, panel * block:(panel + 1) * block]
+            part[:, :, :, at] = result[:, panel * block:(panel + 1) * block].astype(
+                jnp.bfloat16).reshape(2, 2, rows // 4, block)
+
+    half = rows // 4
+    wide = columns // 2
+    own_rows = pl.multiple_of(core * half, half)
+
+    def across(h):
+        return pl.ds(h * wide, wide)
+
+    def core_copy(h):
+        return pltpu.make_async_remote_copy(
+            src_ref=part.at[:, 1 - core, :, across(h)], dst_ref=other.at[:, :, across(h)],
+            send_sem=c_send.at[h], recv_sem=c_recv.at[h], device_id=to_core, device_id_type=MESH)
+
+    def y_copy(h):
+        return pltpu.make_async_remote_copy(
+            src_ref=y_out.at[:, across(h)], dst_ref=y_in.at[:, across(h)],
+            send_sem=y_send.at[h], recv_sem=y_recv.at[h], device_id=to_y, device_id_type=MESH)
+
+    def both_cores(which, h):
+        first = pl.multiple_of(which * 2 * half + own_rows, half)
+        return total[pl.ds(first, half), across(h)] + other[which, :, across(h)].astype(jnp.float32)
+
+    for h in range(2):
+        core_copy(h).start()
+    for h in range(2):
+        core_copy(h).wait_recv()
+        y_out[:, across(h)] = both_cores(1 - run, h).astype(jnp.bfloat16)
+        y_copy(h).start()
+
+    def basis_slot(place, h):
+        return out_ref.at[place * 2 + x, core, :, across(h)]
+
+    def basis_x(place, side, h):
+        ref = out_ref.at[place * 2 + side, core, :, across(h)]
+        return pltpu.make_async_remote_copy(
+            src_ref=ref, dst_ref=ref, send_sem=bx_send.at[place, h],
+            recv_sem=bx_recv.at[place, h], device_id=to_x, device_id_type=MESH)
+
+    def basis_core(at, who, h):
+        ref = out_ref.at[at, who, :, across(h)]
+        return pltpu.make_async_remote_copy(
+            src_ref=ref, dst_ref=ref, send_sem=bc_send.at[at, h],
+            recv_sem=bc_recv.at[at, h], device_id=to_core, device_id_type=MESH)
+
+    def basis_begin(h):
+        y_copy(h).wait_recv()
+        both = both_cores(run, h) + y_in[:, across(h)].astype(jnp.float32)
+        out_ref[tm, core, :, across(h)] = both.astype(jnp.bfloat16)
+
+    def basis_ready(place, h):
+        basis_x(place, x, h).start()
+        basis_core(place * 2 + x, core, h).start()
+
+    basis_sends = line_gather(
+        n_z, z, range(2), basis_slot, to_up, to_down, basis_begin, basis_ready, lambda: None,
+        (b_up, b_down, b_recv))
+    for place in (z, pair, 2 - far, 3 - 3 * far):
+        for h in range(2):
+            basis_x(place, 1 - x, h).wait_recv()
+            basis_core(place * 2 + 1 - x, core, h).start()
+    for h in range(2):
+        for at in range(n_time):
+            basis_core(at, 1 - core, h).wait_recv()
+    frame_copy(run).wait_send()
+    for k in chunks:
+        for place in range(n_z):
+            unless_by_pair(place, k, lambda: panel_x(place, x, k).wait_send())
+    for k in by_pair:
+        panel_pair(z, k).wait_send()
+    panel_sends()
+    basis_sends()
+    for h in range(2):
+        core_copy(h).wait_send()
+        y_copy(h).wait_send()
+        for place in range(n_z):
+            basis_x(place, x, h).wait_send()
+        for at in range(n_time):
+            basis_core(at, core, h).wait_send()
+
+
+def gathered_basis(frames, low, high, n_time):
+    t_local, features = frames.shape
+    width = 2 * low.shape[0] * n_time
+    n_z = n_time // 2
+    half = t_local // 2
+    dma = pltpu.SemaphoreType.DMA
+    vmem = pltpu.VMEM
+    flops = 2 * t_local * features * width
+    return pl.pallas_call(
+        functools.partial(kernel, n_time),
+        out_shape=jax.ShapeDtypeStruct((n_time, 2, half, width), jnp.bfloat16),
+        in_specs=[pl.BlockSpec(memory_space=pl.ANY)] * 3,
+        out_specs=pl.BlockSpec(memory_space=pltpu.VMEM),
+        scratch_shapes=[
+            vmem((2, t_local, features // 2), jnp.bfloat16),
+            vmem((2, n_time, low.shape[0], features // 2), jnp.bfloat16),
+            vmem((2 * t_local, width), jnp.float32),
+            vmem((2, 2, half, width), jnp.bfloat16),
+            vmem((2, half, width), jnp.bfloat16),
+            vmem((half, width), jnp.bfloat16),
+            vmem((half, width), jnp.bfloat16),
+            dma((3,)), dma((1,)), dma((1,)),
+            *[dma((n_z, 4))] * 5, dma((4,)), dma((4,)),
+            *[dma((2,))] * 4,
+            *[dma((n_z, 2))] * 5, dma((n_time, 2)), dma((n_time, 2)),
+        ],
+        compiler_params=pltpu.CompilerParams(
+            collective_id=0, has_side_effects=True, vmem_limit_bytes=56 * 2**20),
+        cost_estimate=pl.CostEstimate(flops=flops, bytes_accessed=16 * 2**20, transcendentals=0),
+    )(frames, low, high)
+
+
+def local(frames, panel_low, panel_high, lags, seg_lengths, ridge):
+    t_local = frames.shape[1]
+    n_time = lax.axis_size("tm")
+    tm, core, run = lax.axis_index("tm"), lax.axis_index("feat"), lax.axis_index("rep")
+    basis = gathered_basis(frames[0], panel_low.T, panel_high.T, n_time)
+    width = basis.shape[-1]
+    total = t_local * n_time
+    basis = basis.reshape(total, width)
+    rows = width // (n_time * 2)
+    lag_most = t_local // 4
+    lag_now = lags[0]
+    positions = jnp.arange(total, dtype=jnp.int32)
+    seg_ends = jnp.cumsum(seg_lengths[0])
+    end_of = jnp.min(
+        jnp.where(seg_ends[None, :] > positions[:, None], seg_ends[None, :], total), axis=1
+    )
+    keep = (positions + lag_now < end_of).astype(jnp.bfloat16)
+
+    def later(values):
+        spare = jnp.zeros((lag_most,) + values.shape[1:], values.dtype)
+        return lax.dynamic_slice_in_dim(
+            jnp.concatenate([spare, values], axis=0), lag_most - lag_now, total, 0)
+
+    later_keep = later(keep)
+    first = (tm * 2 + core) * rows
+    own = lax.dynamic_slice(basis, (0, first), (total, rows))
+    masked = own * keep[:, None]
+    left = jnp.concatenate([masked, later(masked), own * later_keep[:, None]], axis=1)
+    terms = jnp.einsum("ta,tj->aj", left, basis, preferred_element_type=jnp.float32)
+    terms = terms.reshape(3, 2, rows // 2, width)
+    variance = jnp.sum(
+        jnp.square(basis.astype(jnp.float32)) * later_keep.astype(jnp.float32)[:, None], axis=0,
+        keepdims=True)
+    theirs = lax.dynamic_index_in_dim(terms, 1 - run, 1, keepdims=False).reshape(-1, width)
+    mine = lax.dynamic_index_in_dim(terms, run, 1, keepdims=False)
+    received = lax.ppermute(
+        jnp.concatenate([theirs, variance], axis=0), "rep", [(0, 1), (1, 0)])
+    inverse_count = 1.0 / (total * 2)
+    cov_rows = (mine + received[:-1].reshape(mine.shape)) * inverse_count
+    diag_lagged = (variance[0] + received[-1]) * inverse_count
+    return finish(cov_rows, diag_lagged, ridge)
 
 
 def solution(mesh):
@@ -95,4 +449,7 @@
         P(),
     )
     out_specs = (P(None, ("tm", "feat", "rep"), None), P(("tm", "feat", "rep"), None))
-    return jax.shard_map(local, mesh=mesh, in_specs=in_specs, out_specs=out_specs, check_vma=False)
+    shape = dict(mesh.shape)
+    paired = shape["feat"] == 2 and shape["rep"] == 2 and shape["tm"] == 8
+    body = local if paired else local_general
+    return jax.shard_map(body, mesh=mesh, in_specs=in_specs, out_specs=out_specs, check_vma=False)

time: 434 us -> 151 us (0.35)
  waiting for transfers between devices: 350 us -> 11.6 us
  Pallas kernels: 0 us -> 128 us
  blocking collectives: 41 us -> 0 us
  matrix products: 15.8 us -> 2.14 us
  between operations: 14.5 us -> 1.42 us
    all_gather x1 -> x0, waiting for transfers between devices: 230 us -> none  [local(): lax.all_gather(stacked, 'tm', axis=2, tiled=True)]
    pallas_call x0 -> x1, Pallas kernels: none -> 128 us  [gathered_basis(): pl.pallas_call(functools.partial(kernel, n_time), out_shape=jax.ShapeDtyp...]
    reduce_scatter x1 -> x0, waiting for transfers between devices: 97.1 us -> none  [local(): lax.psum_scatter(jnp.stack([term_inst, term_cross, term_lagged], axis=1),...]
    psum x1 -> x0, blocking collectives: 41 us -> none  [local(): diag_lagged = lax.psum(local_var, ('tm', 'rep')) * inverse_count]
    psum x1 -> x0, waiting for transfers between devices: 15.9 us -> none  [local(): lax.psum(partial_rounded, 'feat').astype(jnp.float32).astype(jnp.bfloat16)]
    dot_general x5 -> x2, matrix products: 15.8 us -> 2.14 us  [the longest x1 1.12 us: finish(): jnp.dot(jnp.square(cov_rows[1]), inverse_lagged, precision=lax.Precision....]
    another operation x4 -> x2, other arithmetic: 6.53 us -> 0.2 us  [the longest x1 3.24 us: local(): jnp.stack([term_inst, term_cross, term_lagged], axis=1)]
    ppermute x1, waiting for transfers between devices: 6.47 us -> 11.6 us  [local(): lax.ppermute(jnp.concatenate([theirs, variance], axis=0), 'rep', [(0, 1),...]
  transfers between devices with their start and end apart: 4 -> 1, of which waited for: 4 -> 1; matrix products, arithmetic and copies ran while one was open for 1% -> 0% of each run, Pallas kernels for 0% -> 0%
where the time goes in v1:
time: 151 us
  Pallas kernels  128 us (85%)
  waiting for transfers between devices  11.6 us (8%)
  other arithmetic  6.03 us (4%)
  matrix products  2.14 us (1%)
  local copies, waits for them, and re-layouts  2.01 us (1%)
    pallas_call x1, Pallas kernels, gathered_basis(): pl.pallas_call(functools.partial(kernel, n_time), out_shape=jax.ShapeDtyp...  128 us
    ppermute x1, waiting for transfers between devices, local(): lax.ppermute(jnp.concatenate([theirs, variance], axis=0), 'rep', [(0, 1),...  11.6 us
    reduce_sum x1, other arithmetic, local(): jnp.sum(jnp.square(basis.astype(jnp.float32)) * later_keep.astype(jnp.flo...  3.02 us
  transfers between devices with their start and end apart: 1, of which 1 were waited for; matrix products, arithmetic and copies ran while one was open for 0% of the time, Pallas kernels for 0%

profile of v1, /device:TPU:0, one launch (start us, length us, event | category | flops | bytes accessed | tf_op | source)
XLA Modules:
  0.0 151.3 jit_solution(6021441452074496178)
XLA Ops:
  1.3 0.7 copy.12
  2.0 0.1 reduce-window.8
  2.1 0.1 reduce.1
  2.2 0.2 select_reduce_fusion
  2.4 0.1 pad_dynamic-slice_fusion.1
  2.5 127.5 %shard_map.77 = bf16[8,2,128,1024]{3,2,1,0:T(8,128)(2,1)} custom-call(bf16[256,8192]{1,0:T(8,128)(2,1)} %bitcast.46, bf16[64,8192]{1,0:T(8,128)(2,1)} %bitcast.47, bf16[64,8192]{1,0:T(8,128)(2,1)} %bitcast.48), custom_call_target="tpu_custom_call" | custom-call | flops 4294967296 | bytes 16777216 | tf_op jit(solution)/shard_map/pallas_call | solution.py:375
  130.1 1.8 %dynamic-slice_multiply_fusion.1 = (bf16[2048,64]{1,0:T(8,128)(2,1)S(1)}, bf16[2048,64]{1,0:T(8,128)(2,1)S(1)}) fusion(bf16[2048,1024]{1,0:T(8,128)(2,1)} %bitcast.37, s32[]{:T(128)S(6)} %select_n.18, bf16[2048]{0:T(1024)(128)(2,1)S(1)} %fusion.8, bf16[2048]{0:T(1024)(128)(2,1)S(1)} %pad_dynamic-slice_fusion.1), kind=kLoop, calls=%fused_computation.8 | loop fusion | flops 917504 | bytes 794628 | tf_op jit(solution)/shard_map/mul | solution.py:425
  131.9 0.2 pad_dynamic-slice_fusion
  132.1 0.5 maximum_bitcast_fusion
  132.6 0.5 copy.13
  133.1 0.0 copy-start
  133.1 3.0 %multiply_reduce_fusion = f32[1024]{0:T(1024)S(1)} fusion(bf16[8,2,128,1024]{3,2,1,0:T(8,128)(2,1)} %shard_map.77, f32[8,2,128]{2,1,0:T(2,128)S(1)} %convert.1), kind=kLoop, calls=%fused_computation | loop fusion | flops 8387584 | bytes 4206592 | tf_op jit(solution)/shard_map/reduce_sum | solution.py:429
  136.2 0.4 copy-done
  136.6 0.0 copy-start.2
  136.6 1.0 fusion.10
  137.7 0.5 collective-permute-start
  138.2 11.6 %collective-permute-done = f32[97,1024]{1,0:T(8,128)S(1)} collective-permute-done((f32[97,1024]{1,0:T(8,128)S(1)}, f32[97,1024]{1,0:T(8,128)S(1)}, u32[]{:S(2)}, u32[]{:S(2)}) %collective-permute-start) | collective-permute-done | bytes 397344 | tf_op jit(solution)/shard_map/ppermute | solution.py:434
  149.9 0.1 fusion
  150.0 0.0 copy-start.1
  150.0 0.2 fusion.5
  150.2 0.0 copy-done.2
  150.2 1.1 convolution_divide_fusion
  151.3 0.0 copy-done.1
  (8 shorter events, 0.1 us)
Async XLA Ops:
  133.1 3.5 %copy-start = (bf16[8,2,128,1024]{3,2,1,0:T(8,128)(2,1)S(1)}, bf16[8,2,128,1024]{3,2,1,0:T(8,128)(2,1)}, u32[]{:S(2)}) copy-start(bf16[8,2,128,1024]{3,2,1,0:T(8,128)(2,1)} %shard_map.77) | copy-start | bytes 12582916
  136.6 13.6 %copy-start.2 = (f32[32]{0:T(128)S(1)}, f32[32]{0:T(128)}, u32[]{:S(2)}) copy-start(f32[32]{0:T(128)} %param.11) | copy-start | bytes 388
  137.7 12.2 %collective-permute-start = (f32[97,1024]{1,0:T(8,128)S(1)}, f32[97,1024]{1,0:T(8,128)S(1)}, u32[]{:S(2)}, u32[]{:S(2)}) collective-permute-start(f32[97,1024]{1,0:T(8,128)S(1)} %pad_maximum_fusion), channel_id=1, source_target_pairs={{0,1},{1,0},{2,3},{3,2},{4,5},{5,4},{6,7},{7,6},{8,9},{9,8},{10,11... | collective-permute-start | bytes 1191944 | tf_op jit(solution)/shard_map/ppermute | solution.py:434
  150.0 1.3 copy-start.1
